TPU v7x, 512 devices: a whole 4x8x8 slice. The times are simulated.
512 devices in a mesh: grp: 32 (over x, y), seq: 16 (over z, core).
Axes of the slice: x: 4, y: 8, z: 8, core: 2. Of those that a mesh axis runs over, the one named last changes fastest.
Arguments:
- tokens: bfloat16 [131072, 512], P(('grp', 'seq')), parts along dimension 0, may hold values from -6 to 6
- group_pos: int32 [32768], P('grp'), parts along dimension 0, may hold values from 0 to 4095, as said below
- log_decay: float32 [131072, 16], P(('grp', 'seq')), parts along dimension 0, may hold values from -1 to 0, as said below
- in_weight: bfloat16 [512, 2176], replicated, may hold values from -0.25 to 0.25
- norm_gain: float32 [1024], replicated, may hold values from 0.1 to 1.9
- out_weight: bfloat16 [1024, 512], replicated, may hold values from -0.1875 to 0.1875
- inner_gain: float32 [512], replicated, may hold values from 0.1 to 1.9
- qkv_weight: bfloat16 [16, 512, 192], P('seq'), may hold values from -1 to 1
- attn_out: bfloat16 [16, 64, 512], P('seq'), may hold values from -0.1875 to 0.1875
Outputs:
- result: bfloat16 [131072, 512], P(('grp', 'seq')), parts along dimension 0
There are 32 independent parts, one for each index of `grp`. A program takes and returns all parts, laid end to end along the dimension named above; an argument that names none is the same for every part. Nothing has to cross between parts.
Inputs may be any that keep to these rules, and one draw needn't show every extreme that they name: `group_pos`: strictly increasing. Each device's 256 positions hold at least one group start and at most 128; some device holds exactly 128. `log_decay`: negative at every position.
All inputs are finite; a program needn't handle non-finite values.
Results may differ from a plain program's by a relative error of at most 0.0061.
Values may be sent and summed in bfloat16 or wider, within the bound.
A program may use at most 64 MiB of HBM per device.

v0:
```python
import jax
import jax.numpy as jnp
from jax import lax
from jax.sharding import Mesh
from jax.sharding import PartitionSpec as P

SEQ = ("seq_0", "seq_1")
GRP_SEQ = ("grp", "seq_0", "seq_1")


def nothing_yet(shard, identity):
    return jax.tree.map(
        lambda part, zero: jnp.zeros_like(part) + jnp.asarray(zero, part.dtype), shard, identity
    )


def carried_in(shard, axes, combine, identity):
    before = start = nothing_yet(shard, identity)
    subtotal = shard
    for axis in reversed(axes):
        count, here = (lax.axis_size(axis), lax.axis_index(axis))
        pieces = jax.tree.map(lambda part: lax.all_gather(part, axis), subtotal)
        inside, subtotal = (start, start)
        for k in range(count):
            passed = k < here
            subtotal = combine(subtotal, jax.tree.map(lambda part: part[k], pieces))
            inside = jax.tree.map(lambda new, old: jnp.where(passed, new, old), subtotal, inside)
        before = combine(inside, before)
    return before


def in_blocks(shard, dim, count):
    lengths = shard.shape
    tiles = shard.reshape(*lengths[:dim], count, lengths[dim] // count, *lengths[dim + 1 :])
    return jnp.moveaxis(tiles, dim, 0)


def joined_along(tiles, dim):
    tiles = jnp.moveaxis(tiles, 0, dim)
    lengths = tiles.shape
    return tiles.reshape(*lengths[:dim], lengths[dim] * lengths[dim + 1], *lengths[dim + 2 :])


def turned_blocks(tiles, axes, order):
    inside = tiles.shape[1:]
    result = tiles.reshape(*(lax.axis_size(a) for a in axes), *inside)
    for k in order:
        result = lax.all_to_all(result, axes[k], k, k, tiled=True)
    return result.reshape(-1, *inside)


def stepwise_exchange(shard, axes, order, split_dim, concat_dim):
    tiles = in_blocks(shard, split_dim, lax.axis_size(axes))
    return joined_along(turned_blocks(tiles, axes, order), concat_dim)


def rms_norm(values, gain):
    return values * lax.rsqrt(jnp.mean(values * values, axis=-1, keepdims=True) + 1e-05) * gain


def attend(rows, w_qkv, index, valid):
    head_dim = w_qkv.shape[1] // 3
    qkv = jnp.dot(rows, w_qkv, preferred_element_type=jnp.float32).astype(jnp.bfloat16)
    query = qkv[:, :head_dim]
    keys = qkv[:, head_dim : 2 * head_dim]
    values = qkv[:, 2 * head_dim :]
    count = rows.shape[0]
    block = min(512, count)

    def one_block(start):
        query_block = lax.dynamic_slice_in_dim(query, start, block, 0)
        index_block = lax.dynamic_slice_in_dim(index, start, block, 0)
        scores = jnp.dot(query_block, keys.T, preferred_element_type=jnp.float32) * head_dim ** (
            -0.5
        )
        allowed = (index[None, :] <= index_block[:, None]) & valid[None, :]
        scores = jnp.where(allowed, scores, -jnp.inf)
        top = jnp.max(scores, axis=1, keepdims=True)
        expo = jnp.exp(scores - top)
        probs = (expo / jnp.sum(expo, axis=1, keepdims=True)).astype(jnp.bfloat16)
        return jnp.dot(probs, values, preferred_element_type=jnp.float32).astype(jnp.bfloat16)

    starts = jnp.arange(count // block, dtype=jnp.int32) * block
    return lax.map(one_block, starts).reshape(count, head_dim)


def shards(
    tokens, group_pos, log_decay, in_weight, norm_gain, out_weight, inner_gain, qkv_weight, attn_out
):
    highest = lax.Precision.HIGHEST
    length = tokens.shape[0]
    heads = log_decay.shape[1]
    width = out_weight.shape[0]
    model_width = out_weight.shape[1]
    head_size = width // heads
    state_dim = (in_weight.shape[1] - 2 * width) // 2
    proj = jnp.dot(tokens, in_weight, preferred_element_type=jnp.float32).astype(jnp.bfloat16)
    xs = proj[:, :width].astype(jnp.float32).reshape(length, heads, head_size)
    gate = proj[:, width : 2 * width].astype(jnp.float32)
    bmat = proj[:, 2 * width : 2 * width + state_dim].astype(jnp.float32)
    cmat = proj[:, 2 * width + state_dim :].astype(jnp.float32)
    cumul = jnp.cumsum(log_decay, axis=0)
    differ = cumul.T[:, :, None] - cumul.T[:, None, :]
    lower = jnp.arange(length)[:, None] >= jnp.arange(length)[None, :]
    decays = jnp.exp(jnp.where(lower[None], differ, -jnp.inf))
    intersections = jnp.dot(cmat, bmat.T, precision=highest)
    within = jnp.einsum("hij,jhp->ihp", decays * intersections[None], xs, precision=highest)
    tails = jnp.exp(cumul[-1][None, :] - cumul)
    local_state = jnp.einsum("jh,jhp,jn->hpn", tails, xs, bmat, precision=highest)
    total_decay = jnp.exp(cumul[-1])

    def link(earlier, later):
        return (earlier[0] * later[0], later[0][:, None, None] * earlier[1] + later[1])

    identity = (jnp.ones_like(total_decay), jnp.zeros_like(local_state))
    _, state_in = carried_in((total_decay, local_state), SEQ, link, identity)
    carried = jnp.einsum("ih,in,hpn->ihp", jnp.exp(cumul), cmat, state_in, precision=highest)
    gated = (within + carried).reshape(length, width) * jax.nn.silu(gate)
    normed = rms_norm(gated, norm_gain).astype(jnp.bfloat16)
    hidden = (
        tokens.astype(jnp.float32) + jnp.dot(normed, out_weight, preferred_element_type=jnp.float32)
    ).astype(jnp.bfloat16)
    position = lax.axis_index(SEQ)
    devices = lax.axis_size(SEQ)
    most = length // 2
    groups = group_pos.shape[0]
    starts = jnp.arange(devices, dtype=jnp.int32) * length
    before = jnp.sum((group_pos[None, :] < starts[:, None]).astype(jnp.int32), axis=1)
    upto = jnp.sum((group_pos[None, :] < (starts + length)[:, None]).astype(jnp.int32), axis=1)
    counts = upto - before
    slots = jnp.arange(most, dtype=jnp.int32)
    picks = jnp.clip(before[position] + slots, 0, groups - 1)
    valid_here = slots < counts[position]
    local_pos = group_pos[picks] - position * length
    placing = (
        (local_pos[:, None] == jnp.arange(length, dtype=jnp.int32)[None, :]) & valid_here[:, None]
    ).astype(jnp.float32)
    rows = jnp.dot(placing.astype(jnp.bfloat16), hidden, preferred_element_type=jnp.float32)
    rows_n = rms_norm(rows, inner_gain).astype(jnp.bfloat16)
    gathered = lax.all_gather(rows_n, SEQ, axis=0, tiled=True)
    slot_group = (before[:, None] + slots[None, :]).reshape(-1)
    slot_valid = (slots[None, :] < counts[:, None]).reshape(-1)
    w_qkv = qkv_weight[0]
    owners = group_pos // length
    ordinal = jnp.arange(groups, dtype=jnp.int32)
    index = owners * most + ordinal - before[owners]
    packed = jnp.take(gathered, index, axis=0)
    outputs = attend(packed, w_qkv, ordinal, jnp.ones((groups,), jnp.bool_))
    spread = jnp.take(outputs, jnp.clip(slot_group, 0, groups - 1), axis=0)
    heads_out = jnp.where(slot_valid[:, None], spread, jnp.zeros_like(spread))
    full_out = lax.all_gather(attn_out, SEQ, axis=0, tiled=True)
    mine = stepwise_exchange(heads_out[:, None, :], SEQ, (1, 0), 0, 1)
    back = jnp.dot(
        mine.reshape(most, -1),
        full_out.reshape(-1, model_width),
        preferred_element_type=jnp.float32,
    )
    placed = jnp.dot(placing.T, back, precision=highest)
    return (hidden.astype(jnp.float32) + placed).astype(jnp.bfloat16)


def solution(mesh):
    split = Mesh(mesh.devices.reshape(mesh.shape["grp"], 8, 2), ("grp", "seq_0", "seq_1"))
    return jax.shard_map(
        shards,
        mesh=split,
        in_specs=(
            P(GRP_SEQ, None),
            P("grp"),
            P(GRP_SEQ, None),
            P(),
            P(),
            P(),
            P(),
            P(SEQ, None, None),
            P(SEQ, None, None),
        ),
        out_specs=P(GRP_SEQ, None),
        check_vma=False,
    )
```

profile of v0, /device:TPU:2, one launch (start us, length us, event | category | flops | bytes accessed | tf_op | source)
XLA Modules:
  0.0 190.6 jit_solution(11118988941506550398)
XLA Ops:
  6.5 1.6 copy-done
  8.2 2.0 %convolution_convert_fusion.1 = bf16[256,2176]{0,1:T(8,128)(2,1)S(1)} fusion(bf16[256,512]{1,0:T(8,128)(2,1)} %param.11, bf16[512,2176]{1,0:T(8,128)(2,1)S(1)} %copy-done), kind=kOutput, calls=%fused_computation.17 | convolution fusion | flops 570982400 | bytes 3604480 | tf_op jit(solution)/shard_map/dot_general | solution.py:97
  12.1 1.7 fusion.26
  13.8 2.7 %all-gather = f32[32,64,64]{2,1,0:T(8,128)} all-gather(f32[16,64,64]{2,1,0:T(8,128)S(1)} %fusion.26), channel_id=2, replica_groups=mesh['grp'=32,'seq_0'=8,'seq_1'=2] {'seq_1'}, dimensions={0}, use_global_device_ids=true | all-gather | bytes 786432 | tf_op jit(solution)/shard_map/all_gather | solution.py:22
  16.5 1.8 all-gather.1
  18.3 2.1 %bitcast_add_fusion = f32[1,16,64,64]{3,2,1,0:T(8,128)} fusion(f32[32,64,64]{2,1,0:T(8,128)} %all-gather, f32[16]{0:T(128)S(1)} %get-tuple-element.146, f32[16]{0:T(128)S(1)} %get-tuple-element.148), kind=kLoop, calls=%fused_computation.64 | loop fusion | flops 196608 | bytes 786560 | tf_op jit(solution)/shard_map/add | solution.py:113
  23.7 22.2 %all-gather.2 = f32[8,1,16]{2,1,0:T(1,128)S(1)} all-gather(f32[1,1,16]{2,1,0:T(1,128)S(1)} %get-tuple-element.147), channel_id=1, replica_groups=mesh['grp'=32,'seq_0'=8,'seq_1'=2] {'seq_0'}, dimensions={0}, use_global_device_ids=true | all-gather | bytes 576 | tf_op jit(solution)/shard_map/all_gather | solution.py:22
  46.9 5.4 %fusion.15 = f32[256,16,64]{0,2,1:T(8,128)} fusion(bf16[256,16,64]{0,2,1:T(8,128)(2,1)} %bitcast.189, f32[256,256]{1,0:T(8,128)S(1)} %fusion.110, f32[16,256]{1,0:T(8,128)S(1)} %get-tuple-element.136, pred[256,256]{1,0:T(8,128)(4,1)S(1)} %iota_compare_fusion), kind=kOutput, calls=%fused_computation.23 | convolution fusion | flops 808452096 | bytes 1916928 | tf_op jit(solution)/shard_map/hij,jhp->ihp/dot_general | solution.py:107
  52.2 31.2 %all-gather.7.cloned.1.call-done = f32[8,16,64,64]{3,2,1,0:T(8,128)} async-done(((f32[1,16,64,64]{3,2,1,0:T(8,128)}), f32[8,16,64,64]{3,2,1,0:T(8,128)}) %all-gather.7.cloned.1.call-update) | async-done | bytes 2097168 | tf_op jit(solution)/shard_map/all_gather | solution.py:22
  83.5 4.5 %fusion.18 = f32[256,16,64]{0,2,1:T(8,128)S(1)} fusion(f32[256,16,64]{0,2,1:T(8,128)} %fusion.15, f32[8,16,64,64]{3,2,1,0:T(8,128)} %all-gather.7.cloned.1.call-done, f32[256,16]{0,1:T(8,128)S(1)} %get-tuple-element.133, f32[256,64]{0,1:T(8,128)S(1)} %slice_convert_fusion, f32[32,64,64]{2,1,0:T(8,128)} %all-gather, f32[16]{0:T(128)S(1)} %get-tuple-element.146, ...), kind=kOutput, calls=%fused_computation.25 | convolution fusion | flops 203816960 | bytes 4801226 | tf_op jit(solution)/shard_map/ih,in,hpn->ihp/dot_general | solution.py:117
  92.2 10.1 %compare_and_fusion = (pred[1024]{0:T(1024)(128)(4,1)S(1)}, s32[1024]{0:T(1024)S(1)}) fusion(s32[]{:T(128)} %bitcast.45, s32[]{:T(128)} %bitcast.44, s32[]{:T(128)} %bitcast.43, s32[]{:T(128)} %bitcast.42, s32[]{:T(128)} %bitcast.41, s32[]{:T(128)} %bitcast.40, s32[]{:T(128)} %bitcast.39, s32[]{:T(128)} %bitcast.38, s32[]{:T(128)} %bitcast.37, s32[]{:T(128)} %bitcast.36, ...), kind=kLoop, calls=%fused_computation.165 | loop fusion | flops 58368 | bytes 9280 | tf_op jit(solution)/shard_map/jit(_take)/and | solution.py:147
  102.7 30.0 %all-gather.9.cloned.1.call-done = bf16[2048,512]{1,0:T(8,128)(2,1)} async-done(((bf16[128,512]{1,0:T(8,128)(2,1)}), bf16[2048,512]{1,0:T(8,128)(2,1)}) %all-gather.9.cloned.1.call-update) | async-done | bytes 2097168 | tf_op jit(solution)/shard_map/all_gather | solution.py:140
  132.7 7.0 %gather_fusion.1 = bf16[1024,512]{1,0:T(8,128)(2,1)} fusion(bf16[2048,512]{1,0:T(8,128)(2,1)} %all-gather.9.cloned.1.call-done, s32[1024]{0:T(1024)S(1)} %broadcast_clamp_fusion.1), kind=kCustom, calls=%fused_computation.1 | custom fusion | bytes 2101248 | tf_op jit(solution)/shard_map/jit(_take)/gather | solution.py:147
  139.6 1.8 convolution_convert_fusion.2
  142.5 11.1 %while.11 = (s32[]{:T(128)}, bf16[2,512,64]{1,2,0:T(8,128)(2,1)S(1)}, s32[1024]{0:T(1024)S(1)}, s32[2]{0:T(128)S(1)}, bf16[1024,64]{0,1:T(8,128)(2,1)}, /*index=...) while((s32[]{:T(128)}, ...), condition=%wide.region_9.10_spmd.clone, body=%wide.region_6.9_spmd.clone.sunk | while | flops 138968064 | bytes 6836391 | solution.py:84
  145.3 1.6 fusion.149
  150.9 1.6 fusion.149
  153.8 6.2 %gather_fusion.2 = bf16[2048,64]{1,0:T(8,128)(2,1)S(1)} fusion(bf16[1024,64]{1,0:T(8,128)(2,1)S(1)} %bitcast.186, s32[2048]{0:T(1024)S(1)} %broadcast_clamp_fusion), kind=kCustom, calls=%fused_computation.2 | custom fusion | bytes 532480 | tf_op jit(solution)/shard_map/jit(_take)/gather | solution.py:149
  160.3 3.9 %all_to_all.10 = bf16[8,2,128,1,64]{2,4,3,0,1:T(8,128)(2,1)S(1)} all-to-all(bf16[8,2,128,1,64]{2,4,3,0,1:T(8,128)(2,1)S(1)} %select_select_fusion), channel_id=1, replica_groups=mesh['grp'=32,'seq_0'=8,'seq_1'=2] {'seq_1'}, dimensions={1} | all-to-all | bytes 524288 | tf_op jit(solution)/shard_map/all_to_all | solution.py:48
  165.0 4.2 %all-to-all-start.1 = ((bf16[8,2,128,1,64]{2,4,3,1,0:T(8,128)(2,1)}), bf16[8,2,128,1,64]{2,4,3,1,0:T(8,128)(2,1)S(1)}, u32[]{:S(2)}, u32[]{:S(2)}) async-start(bf16[8,2,128,1,64]{2,4,3,1,0:T(8,128)(2,1)} %copy.84), calls=%async_computation.1 | async-start | bytes 524288 | tf_op jit(solution)/shard_map/all_to_all | solution.py:48
  169.1 5.9 %all-gather.11.cloned.1.call-done = bf16[16,64,512]{2,1,0:T(8,128)(2,1)} async-done(((bf16[1,64,512]{2,1,0:T(8,128)(2,1)}), bf16[16,64,512]{2,1,0:T(8,128)(2,1)}) %all-gather.11.cloned.1.call-update) | async-done | bytes 1048592 | tf_op jit(solution)/shard_map/all_gather | solution.py:151
  175.0 6.3 %all-to-all-done.1 = bf16[8,2,128,1,64]{2,4,3,1,0:T(8,128)(2,1)S(1)} async-done(((bf16[8,2,128,1,64]{2,4,3,1,0:T(8,128)(2,1)}), bf16[8,2,128,1,64]{2,4,3,1,0:T(8,128)(2,1)S(1)}, u32[]{:S(2)}, u32[]{:S(2)}) %all-to-all-start.1) | async-done | bytes 262176 | tf_op jit(solution)/shard_map/all_to_all | solution.py:48
  181.3 1.6 fusion.130
  182.9 1.2 fusion.20
  (81 shorter events, 16.4 us)
Async XLA Ops:
  6.5 1.6 copy-start
  6.5 76.9 %all-gather.7.cloned.1.call-start = ((), (), s32[]{:S(2)}) async-start(), calls=%async_computation.2 | async-start | bytes 4718592 | tf_op jit(solution)/shard_map/all_gather | solution.py:22
  8.2 2.8 %copy-start.4 = (f32[256,16]{0,1:T(8,128)S(1)}, f32[256,16]{0,1:T(8,128)}, u32[]{:S(2)}) copy-start(f32[256,16]{0,1:T(8,128)} %param.13) | copy-start | bytes 49156
  13.8 6.7 %copy-start.1 = (s32[1024]{0:T(1024)S(1)}, s32[1024]{0:T(1024)}, u32[]{:S(2)}) copy-start(s32[1024]{0:T(1024)} %param.12) | copy-start | bytes 12292
  20.4 112.3 %all-gather.9.cloned.1.call-start = ((), (), s32[]{:S(2)}) async-start(), calls=%async_computation.3 | async-start | bytes 2228224 | tf_op jit(solution)/shard_map/all_gather | solution.py:140
  88.0 1.0 copy-start.2
  88.0 1.3 copy-start.3
  88.0 1.3 copy-start.5
  88.4 2.0 %copy-start.6 = (f32[512]{0:T(512)S(1)}, f32[512]{0:T(512)}, u32[]{:S(2)}) copy-start(f32[512]{0:T(512)} %param.17) | copy-start | bytes 6148
  91.2 83.7 %all-gather.11.cloned.1.call-start = ((), (), s32[]{:S(2)}) async-start(), calls=%async_computation.4 | async-start | bytes 1114112 | tf_op jit(solution)/shard_map/all_gather | solution.py:151
  102.7 36.9 %copy-start.7 = (bf16[1,512,192]{1,2,0:T(8,128)(2,1)S(1)}, bf16[1,512,192]{1,2,0:T(8,128)(2,1)}, u32[]{:S(2)}) copy-start(bf16[1,512,192]{1,2,0:T(8,128)(2,1)} %param.18) | copy-start | bytes 589828
  165.0 16.3 %all-to-all-start.1 = ((bf16[8,2,128,1,64]{2,4,3,1,0:T(8,128)(2,1)}), bf16[8,2,128,1,64]{2,4,3,1,0:T(8,128)(2,1)S(1)}, u32[]{:S(2)}, u32[]{:S(2)}) async-start(bf16[8,2,128,1,64]{2,4,3,1,0:T(8,128)(2,1)} %copy.84), calls=%async_computation.1 | async-start | bytes 524288 | tf_op jit(solution)/shard_map/all_to_all | solution.py:48
Sparse Core Ops, SparseCore 0:
  20.6 62.8 all-gather.6
  91.4 41.2 all-gather.8
  134.8 40.1 all-gather.10
where the time goes:
time: 191 us
  waiting for transfers between devices  74.1 us (39%)
  blocking collectives  30.6 us (16%)
  matrix products  23.9 us (13%)
  local copies, waits for them, and re-layouts  23.1 us (12%)
  other arithmetic  17 us (9%)
  between operations  13.4 us (7%)
  starting transfers between devices  4.24 us (2%)
  loops' own time  4.2 us (2%)
    all_gather x1, waiting for transfers between devices, carried_in(): pieces = jax.tree.map(lambda part: lax.all_gather(part, axis), subtotal)  31.2 us
    all_gather x1, waiting for transfers between devices, shards(): gathered = lax.all_gather(rows_n, SEQ, axis=0, tiled=True)  30 us
    all_gather x3, blocking collectives, carried_in(): pieces = jax.tree.map(lambda part: lax.all_gather(part, axis), subtotal)  26.7 us
    and x1, other arithmetic, shards(): packed = jnp.take(gathered, index, axis=0)  10.1 us
    gather x1, local copies, waits for them, and re-layouts, shards(): packed = jnp.take(gathered, index, axis=0)  6.95 us
    gather x2, local copies, waits for them, and re-layouts, shards(): spread = jnp.take(outputs, jnp.clip(slot_group, 0, groups - 1), axis=0)  6.42 us
    all_to_all x1, waiting for transfers between devices, turned_blocks(): result = lax.all_to_all(result, axes[k], k, k, tiled=True)  6.32 us
    all_gather x1, waiting for transfers between devices, shards(): full_out = lax.all_gather(attn_out, SEQ, axis=0, tiled=True)  5.87 us
  transfers between devices with their start and end apart: 4, of which 4 were waited for; matrix products, arithmetic and copies ran while one was open for 23% of the time, Pallas kernels for 0%

commit v1 on v0

--- a/solution.py
+++ b/solution.py
@@ -148,7 +148,9 @@
     outputs = attend(packed, w_qkv, ordinal, jnp.ones((groups,), jnp.bool_))
     spread = jnp.take(outputs, jnp.clip(slot_group, 0, groups - 1), axis=0)
     heads_out = jnp.where(slot_valid[:, None], spread, jnp.zeros_like(spread))
-    full_out = lax.all_gather(attn_out, SEQ, axis=0, tiled=True)
+    full_out = jnp.concatenate(
+        lax.all_to_all(jnp.stack([attn_out] * lax.axis_size(SEQ)), SEQ, 0, 0), axis=0
+    )
     mine = stepwise_exchange(heads_out[:, None, :], SEQ, (1, 0), 0, 1)
     back = jnp.dot(
         mine.reshape(most, -1),

time: 191 us -> 224 us (1.17)
  the two profiles are of different devices: /device:TPU:2 before, /device:TPU:1 now
where the time goes in v1:
time: 224 us; the launch traced here: 223 us
  waiting for transfers between devices  90.6 us (40%)
  blocking collectives  44.3 us (20%)
  local copies, waits for them, and re-layouts  26.7 us (12%)
  matrix products  20.7 us (9%)
  other arithmetic  18.6 us (8%)
  between operations  13.8 us (6%)
  starting transfers between devices  4.68 us (2%)
  loops' own time  3.69 us (2%)
    all_gather x1, waiting for transfers between devices, carried_in(): pieces = jax.tree.map(lambda part: lax.all_gather(part, axis), subtotal)  34.7 us
    all_gather x1, waiting for transfers between devices, shards(): gathered = lax.all_gather(rows_n, SEQ, axis=0, tiled=True)  29.6 us
    all_to_all x1, waiting for transfers between devices, shards(): lax.all_to_all(jnp.stack([attn_out] * lax.axis_size(SEQ)), SEQ, 0, 0)  26.3 us
    all_gather x3, blocking collectives, carried_in(): pieces = jax.tree.map(lambda part: lax.all_gather(part, axis), subtotal)  24.1 us
    all_to_all x2, blocking collectives, turned_blocks(): result = lax.all_to_all(result, axes[k], k, k, tiled=True)  20.2 us
    and x1, other arithmetic, shards(): packed = jnp.take(gathered, index, axis=0)  10.6 us
    gather x2, local copies, waits for them, and re-layouts, shards(): spread = jnp.take(outputs, jnp.clip(slot_group, 0, groups - 1), axis=0)  6.42 us
    gather x1, local copies, waits for them, and re-layouts, shards(): packed = jnp.take(gathered, index, axis=0)  5.85 us
  transfers between devices with their start and end apart: 3, of which 3 were waited for; matrix products, arithmetic and copies ran while one was open for 10% of the time, Pallas kernels for 0%

profile of v1, /device:TPU:1, one launch (start us, length us, event | category | flops | bytes accessed | tf_op | source)
XLA Modules:
  0.0 223.1 jit_solution(13182242072250976446)
XLA Ops:
  6.5 1.6 copy-done
  8.2 2.0 convolution_convert_fusion.1
  12.1 1.7 fusion.27
  13.8 9.2 %all-gather = f32[32,64,64]{2,1,0:T(8,128)} all-gather(f32[16,64,64]{2,1,0:T(8,128)S(1)} %fusion.27), channel_id=2, replica_groups=mesh['grp'=32,'seq_0'=8,'seq_1'=2] {'seq_1'}, dimensions={0}, use_global_device_ids=true | all-gather | bytes 786432 | tf_op jit(solution)/shard_map/all_gather | solution.py:22
  23.0 1.8 all-gather.1
  24.8 2.1 bitcast_add_fusion
  30.3 13.1 %all-gather.2 = f32[8,1,16]{2,1,0:T(1,128)S(1)} all-gather(f32[1,1,16]{2,1,0:T(1,128)S(1)} %get-tuple-element.147), channel_id=1, replica_groups=mesh['grp'=32,'seq_0'=8,'seq_1'=2] {'seq_0'}, dimensions={0}, use_global_device_ids=true | all-gather | bytes 576 | tf_op jit(solution)/shard_map/all_gather | solution.py:22
  44.3 5.4 %fusion.15 = f32[256,16,64]{0,2,1:T(8,128)} fusion(bf16[256,16,64]{0,2,1:T(8,128)(2,1)} %bitcast.193, f32[256,256]{1,0:T(8,128)S(1)} %fusion.111, f32[16,256]{1,0:T(8,128)S(1)} %get-tuple-element.136, pred[256,256]{1,0:T(8,128)(4,1)S(1)} %iota_compare_fusion), kind=kOutput, calls=%fused_computation.23 | convolution fusion | flops 808452096 | bytes 1916928 | tf_op jit(solution)/shard_map/hij,jhp->ihp/dot_general | solution.py:107
  49.7 34.7 %all-gather.6.cloned.1.call-done = f32[8,16,64,64]{3,2,1,0:T(8,128)} async-done(((f32[1,16,64,64]{3,2,1,0:T(8,128)}), f32[8,16,64,64]{3,2,1,0:T(8,128)}) %all-gather.6.cloned.1.call-update) | async-done | bytes 2097168 | tf_op jit(solution)/shard_map/all_gather | solution.py:22
  84.3 4.5 %fusion.18 = f32[256,16,64]{0,2,1:T(8,128)S(1)} fusion(f32[256,16,64]{0,2,1:T(8,128)} %fusion.15, f32[8,16,64,64]{3,2,1,0:T(8,128)} %all-gather.6.cloned.1.call-done, f32[256,16]{0,1:T(8,128)S(1)} %get-tuple-element.133, f32[256,64]{0,1:T(8,128)S(1)} %slice_convert_fusion, f32[32,64,64]{2,1,0:T(8,128)} %all-gather, f32[16]{0:T(128)S(1)} %get-tuple-element.146, ...), kind=kOutput, calls=%fused_computation.25 | convolution fusion | flops 203816960 | bytes 4801226 | tf_op jit(solution)/shard_map/ih,in,hpn->ihp/dot_general | solution.py:117
  93.7 10.6 %compare_and_fusion = (pred[1024]{0:T(1024)(128)(4,1)}, s32[1024]{0:T(1024)S(1)}) fusion(s32[]{:T(128)} %bitcast.45, s32[]{:T(128)} %bitcast.44, s32[]{:T(128)} %bitcast.43, s32[]{:T(128)} %bitcast.42, s32[]{:T(128)} %bitcast.41, s32[]{:T(128)} %bitcast.40, s32[]{:T(128)} %bitcast.39, s32[]{:T(128)} %bitcast.38, s32[]{:T(128)} %bitcast.37, s32[]{:T(128)} %bitcast.36, ...), kind=kLoop, calls=%fused_computation.167 | loop fusion | flops 58368 | bytes 9280 | tf_op jit(solution)/shard_map/jit(_take)/and | solution.py:147
  104.4 29.6 %all-gather.8.cloned.1.call-done = bf16[2048,512]{1,0:T(8,128)(2,1)} async-done(((bf16[128,512]{1,0:T(8,128)(2,1)}), bf16[2048,512]{1,0:T(8,128)(2,1)}) %all-gather.8.cloned.1.call-update) | async-done | bytes 2097168 | tf_op jit(solution)/shard_map/all_gather | solution.py:140
  134.0 5.8 %gather_fusion.1 = bf16[1024,512]{1,0:T(8,128)(2,1)S(1)} fusion(bf16[2048,512]{1,0:T(8,128)(2,1)} %all-gather.8.cloned.1.call-done, s32[1024]{0:T(1024)S(1)} %broadcast_clamp_fusion.1), kind=kCustom, calls=%fused_computation.1 | custom fusion | bytes 2101248 | tf_op jit(solution)/shard_map/jit(_take)/gather | solution.py:147
  139.9 1.5 convolution_convert_fusion.2
  141.8 11.4 %while.11 = (s32[]{:T(128)}, bf16[2,512,64]{1,2,0:T(8,128)(2,1)}, s32[1024]{0:T(1024)S(1)}, s32[2]{0:T(128)}, bf16[1024,64]{0,1:T(8,128)(2,1)S(1)}, /*index=5*/b...) while((s32[]{:T(128)}, bf16[2,512,64]{1,2,0:T(8,128)(2,1)}, ...), condition=%wide.region_9.10_spmd.clone, body=%wide.region_6.9_spmd.clone.sunk | while | flops 138968064 | bytes 8016095 | solution.py:84
  141.8 1.2 dynamic_slice.30
  147.5 1.2 dynamic_slice.30
  154.3 6.2 %gather_fusion.2 = bf16[2048,64]{1,0:T(8,128)(2,1)S(1)} fusion(bf16[1024,64]{1,0:T(8,128)(2,1)S(1)} %bitcast.190, s32[2048]{0:T(1024)S(1)} %broadcast_clamp_fusion), kind=kCustom, calls=%fused_computation.2 | custom fusion | bytes 532480 | tf_op jit(solution)/shard_map/jit(_take)/gather | solution.py:149
  160.8 4.6 %all_to_all.15 = bf16[8,2,128,1,64]{2,4,0,3,1:T(8,128)(2,1)} all-to-all(bf16[8,2,128,1,64]{2,4,0,3,1:T(8,128)(2,1)S(1)} %select_select_fusion), channel_id=1, replica_groups=mesh['grp'=32,'seq_0'=8,'seq_1'=2] {'seq_1'}, dimensions={1} | all-to-all | bytes 524288 | tf_op jit(solution)/shard_map/all_to_all | solution.py:48
  166.5 4.6 %all-to-all-start.2 = ((bf16[16,1,64,512]{3,2,1,0:T(8,128)(2,1)}), bf16[16,1,64,512]{3,2,1,0:T(8,128)(2,1)S(1)}, u32[]{:S(2)}, u32[]{:S(2)}) async-start(bf16[16,1,64,512]{3,2,1,0:T(8,128)(2,1)} %stack.2), calls=%async_computation.2 | async-start | bytes 2097152 | tf_op jit(solution)/shard_map/all_to_all | solution.py:152
  171.1 1.7 copy.83
  172.8 26.3 %all-to-all-done.2 = bf16[16,1,64,512]{3,2,1,0:T(8,128)(2,1)S(1)} async-done(((bf16[16,1,64,512]{3,2,1,0:T(8,128)(2,1)}), bf16[16,1,64,512]{3,2,1,0:T(8,128)(2,1)S(1)}, u32[]{:S(2)}, u32[]{:S(2)}) %all-to-all-start.2) | async-done | bytes 1048608 | tf_op jit(solution)/shard_map/all_to_all | solution.py:152
  199.1 15.7 %all_to_all.16 = bf16[8,2,128,1,64]{2,4,1,3,0:T(8,128)(2,1)S(1)} all-to-all(bf16[8,2,128,1,64]{2,4,1,3,0:T(8,128)(2,1)} %copy.83), channel_id=1, replica_groups=mesh['grp'=32,'seq_0'=8,'seq_1'=2] {'seq_0'}, dimensions={0} | all-to-all | bytes 524288 | tf_op jit(solution)/shard_map/all_to_all | solution.py:48
  215.1 1.2 fusion.20
  (98 shorter events, 19.4 us)
Async XLA Ops:
  6.5 1.6 copy-start
  6.5 77.8 %all-gather.6.cloned.1.call-start = ((), (), s32[]{:S(2)}) async-start(), calls=%async_computation.3 | async-start | bytes 4718592 | tf_op jit(solution)/shard_map/all_gather | solution.py:22
  8.2 2.8 %copy-start.7 = (f32[256,16]{0,1:T(8,128)S(1)}, f32[256,16]{0,1:T(8,128)}, u32[]{:S(2)}) copy-start(f32[256,16]{0,1:T(8,128)} %param.13) | copy-start | bytes 49156
  13.8 13.3 %copy-start.1 = (s32[1024]{0:T(1024)S(1)}, s32[1024]{0:T(1024)}, u32[]{:S(2)}) copy-start(s32[1024]{0:T(1024)} %param.12) | copy-start | bytes 12292
  27.0 107.0 %all-gather.8.cloned.1.call-start = ((), (), s32[]{:S(2)}) async-start(), calls=%async_computation.4 | async-start | bytes 2228224 | tf_op jit(solution)/shard_map/all_gather | solution.py:140
  44.0 47.0 %copy-start.11 = (pred[128]{0:T(512)(128)(4,1)}, pred[128]{0:T(512)(128)(4,1)S(1)}, u32[]{:S(2)}) copy-start(pred[128]{0:T(512)(128)(4,1)S(1)} %iota_compare_fusion.3) | copy-start | bytes 388
  44.1 46.9 %copy-start.13 = (s32[128]{0:T(128)}, s32[128]{0:T(128)S(1)}, u32[]{:S(2)}) copy-start(s32[128]{0:T(128)S(1)} %broadcast_subtract_fusion) | copy-start | bytes 1540
  88.9 1.0 copy-start.2
  88.9 1.3 copy-start.3
  88.9 1.3 copy-start.9
  89.3 2.0 copy-start.10
  144.9 1.3 copy-start.4
  146.9 0.7 copy-start.5
  150.6 1.3 copy-start.4
  152.6 0.7 copy-start.5
  154.3 6.5 %copy-start.8 = (pred[8,2,128]{2,0,1:T(8,128)(4,1)S(1)}, pred[8,2,128]{2,0,1:T(8,128)(4,1)}, u32[]{:S(2)}) copy-start(pred[8,2,128]{2,0,1:T(8,128)(4,1)} %iota_compare_fusion.2) | copy-start | bytes 6148
  154.3 11.1 %copy-start.6 = (bf16[1,64,512]{2,1,0:T(8,128)(2,1)S(1)}, bf16[1,64,512]{2,1,0:T(8,128)(2,1)}, u32[]{:S(2)}) copy-start(bf16[1,64,512]{2,1,0:T(8,128)(2,1)} %param.19) | copy-start | bytes 196612
  166.5 48.6 %copy-start.12 = (pred[128]{0:T(512)(128)(4,1)S(1)}, pred[128]{0:T(512)(128)(4,1)}, u32[]{:S(2)}) copy-start(pred[128]{0:T(512)(128)(4,1)} %copy-done.11) | copy-start | bytes 388
  166.5 48.6 %copy-start.14 = (s32[128]{0:T(128)S(1)}, s32[128]{0:T(128)}, u32[]{:S(2)}) copy-start(s32[128]{0:T(128)} %copy-done.13) | copy-start | bytes 1540
  166.5 32.6 %all-to-all-start.2 = ((bf16[16,1,64,512]{3,2,1,0:T(8,128)(2,1)}), bf16[16,1,64,512]{3,2,1,0:T(8,128)(2,1)S(1)}, u32[]{:S(2)}, u32[]{:S(2)}) async-start(bf16[16,1,64,512]{3,2,1,0:T(8,128)(2,1)} %stack.2), calls=%async_computation.2 | async-start | bytes 2097152 | tf_op jit(solution)/shard_map/all_to_all | solution.py:152
Sparse Core Ops, SparseCore 0:
  27.1 57.1 all-gather.5
  92.2 41.7 all-gather.7
